TPU v7x, 128 devices: a whole 4x4x4 slice. The times are simulated.
128 devices in a mesh: inst: 8 (over y_hi, z), tile: 16 (over y_lo, x, core).
Axes of the slice: x: 4, y: 4 (y_hi: 2, y_lo: 2; y = y_hi * 2 + y_lo), z: 4, core: 2. Of those that a mesh axis runs over, the one named last changes fastest.
Arguments:
- magnetic: float32 [8, 3, 4, 1024, 1024], P('inst', None, None, 'tile'), may hold values from -6 to 6
- velocity: float32 [8, 3, 4, 1024, 1024], P('inst', None, None, 'tile'), may hold values from -6 to 6
Outputs:
- residual: float32 [8, 3, 4, 1024, 1024], P('inst', None, None, 'tile')
All inputs are finite; a program needn't handle non-finite values.
Results may differ from a plain program's by a relative error of at most 0.000055.
Values sent between devices are 32-bit elements; how exact they have to be, the bound alone decides.
A program may use at most 192 MiB of HBM per device.

v0:
```python
import jax
import jax.numpy as jnp
from jax import lax
from jax.sharding import PartitionSpec as P

RESIST = 0.2
TIME_DAMP = 0.5


def with_halo(cells, sides, width):
    for axis, dim in sides:
        count = lax.axis_size(axis)
        head = lax.slice_in_dim(cells, 0, width, axis=dim)
        tail = lax.slice_in_dim(cells, cells.shape[dim] - width, cells.shape[dim], axis=dim)
        cells = jnp.concatenate(
            [
                lax.ppermute(tail, axis, [(i, (i + 1) % count) for i in range(count)]),
                cells,
                lax.ppermute(head, axis, [((i + 1) % count, i) for i in range(count)]),
            ],
            axis=dim,
        )
    return cells


def time_weights(inst_count):
    instance = jnp.arange(inst_count, dtype=jnp.int32)
    offset = instance[:, None] - instance[None, :]
    phase_angle = jnp.pi * offset.astype(jnp.float32) / inst_count
    parity = (1 - 2 * (jnp.abs(offset) % 2)).astype(jnp.float32)
    off_diagonal = offset != 0
    safe_sine = jnp.where(off_diagonal, jnp.sin(phase_angle), jnp.ones_like(phase_angle))
    first_part = 0.5 * parity * jnp.cos(phase_angle) / safe_sine
    second_part = -0.5 * parity / (safe_sine * safe_sine)
    second_diag = jnp.full_like(phase_angle, -(inst_count * inst_count + 2) / 12.0)
    first_mat = jnp.where(off_diagonal, first_part, jnp.zeros_like(phase_angle))
    second_mat = jnp.where(off_diagonal, second_part, second_diag)
    return first_mat - TIME_DAMP * second_mat


def deriv_axis(values, axis):
    return (jnp.roll(values, -1, axis) - jnp.roll(values, 1, axis)) * 0.5


def second_axis(values, axis):
    return jnp.roll(values, -1, axis) + jnp.roll(values, 1, axis) - 2.0 * values


def induction(field_b, flow_u):
    emf_x = flow_u[1] * field_b[2] - flow_u[2] * field_b[1]
    emf_y = flow_u[2] * field_b[0] - flow_u[0] * field_b[2]
    emf_z = flow_u[0] * field_b[1] - flow_u[1] * field_b[0]
    stacked = jnp.concatenate([jnp.stack([emf_x, emf_y, emf_z]), field_b], axis=0)
    extended = with_halo(stacked, (("tile", 2),), 1)
    forward_cells = extended[:, :, 2:, :]
    backward_cells = extended[:, :, :-2, :]
    x_deriv = (forward_cells - backward_cells) * 0.5
    curl_terms = jnp.stack(
        [
            deriv_axis(emf_z, 2) - deriv_axis(emf_y, 0),
            deriv_axis(emf_x, 0) - x_deriv[2],
            x_deriv[1] - deriv_axis(emf_x, 2),
        ]
    )
    x_second = forward_cells[3:] + backward_cells[3:] - 2.0 * field_b
    laplace = second_axis(field_b, 1) + x_second + second_axis(field_b, 3)
    return curl_terms + RESIST * laplace


def per_device(magnetic, velocity):
    inst_count = lax.axis_size("inst")
    own_index = lax.axis_index("inst")
    matrix = time_weights(inst_count)
    induced = induction(magnetic[0], velocity[0])[None]
    own_row = lax.dynamic_index_in_dim(matrix, own_index, 0, keepdims=False)
    derivative = jnp.einsum(
        "m,mczxy->czxy",
        own_row,
        lax.all_gather(magnetic, "inst", axis=0, tiled=True),
        precision=lax.Precision.HIGHEST,
    )[None]
    return derivative - induced


def solution(mesh):
    in_specs = (P("inst", None, None, "tile", None), P("inst", None, None, "tile", None))
    out_specs = P("inst", None, None, "tile", None)
    return jax.shard_map(
        per_device, mesh=mesh, in_specs=in_specs, out_specs=out_specs, check_vma=False
    )
```

profile of v0, /device:TPU:2, one launch (start us, length us, event | category | flops | bytes accessed | tf_op | source)
XLA Modules:
  0.0 329.4 jit_solution(17304772441266254193)
XLA Ops:
  6.5 0.0 copy-start
  6.5 0.0 all-gather.2.cloned.1.call-start
  6.5 0.7 all-gather.2.cloned.1.call-update
  7.3 1.2 copy-done
  8.4 2.9 multiply_subtract_fusion.1
  11.3 0.0 copy-start.1
  11.3 0.0 copy-start.4
  11.3 0.0 copy-start.7
  11.4 1.1 pad_maximum_fusion.4
  12.5 0.0 copy-done.1
  12.5 0.3 copy-done.4
  12.7 0.3 copy-done.7
  13.1 0.0 collective-permute-start
  13.1 0.5 collective-permute-start.1
  13.6 0.0 copy-start.5
  13.6 1.1 slice_bitcast_fusion.14
  14.7 1.1 slice_bitcast_fusion.10
  15.8 1.5 slice_bitcast_fusion.6
  17.3 0.0 copy-done.5
  17.3 0.4 slice_bitcast_fusion.2
  17.7 0.0 copy-start.2
  17.7 1.5 fusion.12
  19.2 0.0 copy-done.2
  19.2 0.8 slice_bitcast_fusion.12
  20.0 1.0 fusion.24
  21.0 1.3 fusion.26
  22.3 1.3 slice_bitcast_fusion.4
  23.7 1.7 slice_bitcast_fusion
  25.4 3.3 %fusion.27 = (f32[3,3,64,1024]{3,2,1,0:T(8,128)}, f32[3,3,64,1024]{3,2,1,0:T(8,128)}) fusion(f32[3,4,64,1024]{3,2,1,0:T(8,128)S(1)} %bitcast.52), kind=kLoop, calls=%fused_computation.68 | loop fusion | bytes 9437184 | tf_op jit(solution)/shard_map/jit(_roll_static)/slice | solution.py:46
  28.7 0.0 copy-start.8
  28.7 4.0 %fusion.25 = (f32[3,4,64,1023]{3,2,1,0:T(8,128)}, f32[3,4,64,1023]{3,2,1,0:T(8,128)}) fusion(f32[3,4,64,1024]{3,2,1,0:T(8,128)S(1)} %bitcast.53), kind=kLoop, calls=%fused_computation.66 | loop fusion | bytes 12570624 | tf_op jit(solution)/shard_map/jit(_roll_static)/slice | solution.py:46
  32.7 0.1 multiply_subtract_fusion.4
  32.7 0.0 collective-permute-done
  32.7 0.0 collective-permute-done.1
  32.7 0.0 copy-done.8
  32.8 2.7 pad_maximum_fusion
  35.5 4.3 %fusion.2 = f32[6,4,64,1024]{3,2,1,0:T(8,128)} fusion(f32[6,4,65,1024]{3,2,1,0:T(8,128)S(1)} %get-tuple-element.8, f32[6,4,65,1024]{3,2,1,0:T(8,128)S(1)} %get-tuple-element.7), kind=kLoop, calls=%fused_computation.5 | loop fusion | flops 3145728 | bytes 18874368 | tf_op jit(solution)/shard_map/mul | solution.py:57
  39.8 4.6 %slice_subtract_fusion.2 = (f32[1,4,64,1024]{3,2,1,0:T(8,128)}, f32[1,4,64,1024]{3,2,1,0:T(8,128)}) fusion(f32[6,4,64,1024]{3,2,1,0:T(8,128)} %fusion.2, f32[1,1,64,1024]{3,2,1,0:T(8,128)S(1)} %get-tuple-element.31, f32[1,3,64,1024]{3,2,1,0:T(8,128)} %get-tuple-element.33, f32[1,3,64,1024]{3,2,1,0:T(8,128)} %get-tuple-element.32, ...), kind=kLoop, calls=%fused_computation.21 | loop fusion | flops 2621440 | bytes 8388608 | tf_op jit(solution)/shard_map/sub | solution.py:61
  44.4 226.3 %all-gather.2.cloned.1.call-done = f32[8,3,4,64,1024]{4,3,2,1,0:T(8,128)} async-done(((f32[1,3,4,64,1024]{4,3,2,1,0:T(8,128)}), f32[8,3,4,64,1024]{4,3,2,1,0:T(8,128)}) %all-gather.2.cloned.1.call-update) | async-done | bytes 25165840 | tf_op jit(solution)/shard_map/all_gather | solution.py:79
  270.7 0.0 copy-start.3
  270.7 0.0 copy-start.6
  270.7 0.0 copy-start.9
  270.7 0.0 copy-start.10
  270.7 0.0 copy-start.11
  270.7 0.0 copy-start.12
  270.7 0.0 copy-start.13
  270.7 43.3 %fusion = f32[1,3,4,64,1024]{4,0,3,2,1:T(1,128)} fusion(f32[8,3,4,64,1024]{4,3,2,1,0:T(8,128)} %all-gather.2.cloned.1.call-done, f32[8,8]{1,0:T(8,128)S(1)} %multiply_subtract_fusion.4, s32[]{:T(128)S(6)} %select_n.25), kind=kOutput, calls=%fused_computation | convolution fusion | flops 75497472 | bytes 28312068 | tf_op jit(solution)/shard_map/m,mczxy->czxy/dot_general | solution.py:76
  314.0 0.0 copy-done.3
  314.0 0.0 copy-done.6
  314.0 0.0 copy-done.9
  314.0 0.0 copy-done.10
  314.1 0.0 copy-done.11
  314.1 0.0 copy-done.12
  314.1 0.0 copy-done.13
  314.1 8.4 %fusion.9 = f32[1,3,4,64,1024]{4,3,2,1,0:T(8,128)} fusion(f32[6,4,1,1024]{3,2,1,0:T(1,128)} %collective-permute-done.1, f32[3,4,64,1024]{3,2,1,0:T(8,128)S(1)} %bitcast.55, f32[1,4,64,1024]{3,2,1,0:T(8,128)S(1)} %bitcast.65, f32[1,4,64,1024]{3,2,1,0:T(8,128)S(1)} %bitcast.68, f32[1,4,64,1024]{3,2,1,0:T(8,128)S(1)} %bitcast.60, ...), kind=kLoop, calls=%fused_computation.13 | loop fusion | flops 20447232 | bytes 28508160 | tf_op jit(solution)/shard_map/sub | solution.py:82
  (1 shorter events, 0.0 us)
Async XLA Ops:
  6.5 1.9 copy-start
  6.5 264.2 %all-gather.2.cloned.1.call-start = ((), (), s32[]{:S(2)}) async-start(), calls=%async_computation | async-start | bytes 28311552 | tf_op jit(solution)/shard_map/all_gather | solution.py:79
  11.3 1.1 copy-start.1
  11.3 1.4 copy-start.4
  11.3 1.7 copy-start.7
  13.1 19.7 %collective-permute-start = (f32[6,4,1,1024]{3,2,1,0:T(1,128)}, f32[6,4,1,1024]{3,2,1,0:T(1,128)}, u32[]{:S(2)}, u32[]{:S(2)}) collective-permute-start(f32[6,4,1,1024]{3,2,1,0:T(1,128)} %get-tuple-element.9), channel_id=1, source_target_pairs={{1,0},{2,1},{3,2},{4,3},{5,4},{6,5},{7,6},{8,7},{9,8},{10,9},{11,1... | collective-permute-start | bytes 294920 | tf_op jit(solution)/shard_map/ppermute | solution.py:19
  13.1 19.7 %collective-permute-start.1 = (f32[6,4,1,1024]{3,2,1,0:T(1,128)}, f32[6,4,1,1024]{3,2,1,0:T(1,128)}, u32[]{:S(2)}, u32[]{:S(2)}) collective-permute-start(f32[6,4,1,1024]{3,2,1,0:T(1,128)} %get-tuple-element.10), channel_id=1, source_target_pairs={{0,1},{1,2},{2,3},{3,4},{4,5},{5,6},{6,7},{7,8},{8,9},{9,10},{10,1... | collective-permute-start | bytes 294920 | tf_op jit(solution)/shard_map/ppermute | solution.py:17
  13.6 3.7 %copy-start.5 = (f32[1,1,4,64,1024]{4,3,2,1,0:T(8,128)S(1)}, f32[1,1,4,64,1024]{4,3,2,1,0:T(8,128)}, u32[]{:S(2)}) copy-start(f32[1,1,4,64,1024]{4,3,2,1,0:T(8,128)} %copy-done.4) | copy-start | bytes 3145732
  17.7 1.5 copy-start.2
  28.7 4.1 %copy-start.8 = (f32[1,1,4,64,1024]{4,3,2,1,0:T(8,128)S(1)}, f32[1,1,4,64,1024]{4,3,2,1,0:T(8,128)}, u32[]{:S(2)}) copy-start(f32[1,1,4,64,1024]{4,3,2,1,0:T(8,128)} %copy-done.7) | copy-start | bytes 3145732
  270.7 43.3 %copy-start.3 = (f32[1,1,4,64,1024]{4,3,2,1,0:T(8,128)S(1)}, f32[1,1,4,64,1024]{4,3,2,1,0:T(8,128)}, u32[]{:S(2)}) copy-start(f32[1,1,4,64,1024]{4,3,2,1,0:T(8,128)} %copy-done.1) | copy-start | bytes 3145732
  270.7 43.3 %copy-start.6 = (f32[1,1,4,64,1024]{4,3,2,1,0:T(8,128)S(1)}, f32[1,1,4,64,1024]{4,3,2,1,0:T(8,128)}, u32[]{:S(2)}) copy-start(f32[1,1,4,64,1024]{4,3,2,1,0:T(8,128)} %copy-done.4) | copy-start | bytes 3145732
  270.7 43.3 %copy-start.9 = (f32[1,1,4,64,1024]{4,3,2,1,0:T(8,128)S(1)}, f32[1,1,4,64,1024]{4,3,2,1,0:T(8,128)}, u32[]{:S(2)}) copy-start(f32[1,1,4,64,1024]{4,3,2,1,0:T(8,128)} %copy-done.7) | copy-start | bytes 3145732
  270.7 43.4 %copy-start.10 = (f32[3,4,64,1023]{3,2,1,0:T(8,128)S(1)}, f32[3,4,64,1023]{3,2,1,0:T(8,128)}, u32[]{:S(2)}) copy-start(f32[3,4,64,1023]{3,2,1,0:T(8,128)} %get-tuple-element.16) | copy-start | bytes 9427972
  270.7 43.4 %copy-start.11 = (f32[3,4,64,1023]{3,2,1,0:T(8,128)S(1)}, f32[3,4,64,1023]{3,2,1,0:T(8,128)}, u32[]{:S(2)}) copy-start(f32[3,4,64,1023]{3,2,1,0:T(8,128)} %get-tuple-element.17) | copy-start | bytes 9427972
  270.7 43.4 %copy-start.12 = (f32[1,4,64,1024]{3,2,1,0:T(8,128)S(1)}, f32[1,4,64,1024]{3,2,1,0:T(8,128)}, u32[]{:S(2)}) copy-start(f32[1,4,64,1024]{3,2,1,0:T(8,128)} %get-tuple-element.5) | copy-start | bytes 3145732
  270.7 43.4 %copy-start.13 = (f32[3,1,64,1024]{3,2,1,0:T(8,128)S(1)}, f32[3,1,64,1024]{3,2,1,0:T(8,128)}, u32[]{:S(2)}) copy-start(f32[3,1,64,1024]{3,2,1,0:T(8,128)} %get-tuple-element.18) | copy-start | bytes 2359300
Sparse Core Ops, SparseCore 0:
  9.7 260.9 all-gather.1
where the time goes:
time: 330 us; the launch traced here: 329 us
  waiting for transfers between devices  227 us (69%)
  matrix products  43.3 us (13%)
  other arithmetic  25.6 us (8%)
  local copies, waits for them, and re-layouts  19.4 us (6%)
  between operations  13.6 us (4%)
    all_gather x1, waiting for transfers between devices, per_device(): lax.all_gather(magnetic, 'inst', axis=0, tiled=True)  226 us
    dot_general x1, matrix products, per_device(): jnp.einsum('m,mczxy->czxy', own_row, lax.all_gather(magnetic, 'inst', axi...  43.3 us
    slice x4, local copies, waits for them, and re-layouts, second_axis(): return jnp.roll(values, -1, axis) + jnp.roll(values, 1, axis) - 2.0 * values  9.63 us
    sub x1, other arithmetic, per_device(): return derivative - induced  8.43 us
    concatenate x8, local copies, waits for them, and re-layouts, deriv_axis(): return (jnp.roll(values, -1, axis) - jnp.roll(values, 1, axis)) * 0.5  7.93 us
  transfers between devices with their start and end apart: 3, of which 1 were waited for; matrix products, arithmetic and copies ran while one was open for 11% of the time, Pallas kernels for 0%

commit v1 on v0

--- a/solution.py
+++ b/solution.py
@@ -69,17 +69,15 @@
 
 def per_device(magnetic, velocity):
     inst_count = lax.axis_size("inst")
-    own_index = lax.axis_index("inst")
     matrix = time_weights(inst_count)
-    induced = induction(magnetic[0], velocity[0])[None]
-    own_row = lax.dynamic_index_in_dim(matrix, own_index, 0, keepdims=False)
-    derivative = jnp.einsum(
-        "m,mczxy->czxy",
-        own_row,
-        lax.all_gather(magnetic, "inst", axis=0, tiled=True),
-        precision=lax.Precision.HIGHEST,
-    )[None]
-    return derivative - induced
+    induced = induction(magnetic[0], velocity[0])
+    comps, planes, rows, lanes = induced.shape
+    part = rows // inst_count
+    pieces = magnetic[0].reshape(comps, planes, inst_count, part, lanes)
+    gathered = lax.all_to_all(pieces, "inst", 2, 0, tiled=False)
+    mixed = jnp.einsum("nm,mczxy->nczxy", matrix, gathered, precision=lax.Precision.HIGHEST)
+    derivative = lax.all_to_all(mixed, "inst", 0, 2, tiled=False)
+    return (derivative.reshape(induced.shape) - induced)[None]
 
 
 def solution(mesh):

time: 330 us -> 114 us (0.35)
  waiting for transfers between devices: 227 us -> 38.7 us
  matrix products: 43.3 us -> 6.33 us
  between operations: 13.6 us -> 0.32 us
  starting transfers between devices: 0.51 us -> 13.5 us
  local copies, waits for them, and re-layouts: 19.4 us -> 26.6 us
    all_gather x1 -> x0, waiting for transfers between devices: 226 us -> none  [per_device(): lax.all_gather(magnetic, 'inst', axis=0, tiled=True)]
    all_to_all x0 -> x2, waiting for transfers between devices: none -> 38.7 us  [the longest x1 21.5 us: per_device(): gathered = lax.all_to_all(pieces, 'inst', 2, 0, tiled=False)]
    dot_general x1, matrix products: 43.3 us -> 6.33 us  [per_device(): jnp.einsum('nm,mczxy->nczxy', matrix, gathered, precision=lax.Precision.H...]
    all_to_all x0 -> x2, starting transfers between devices: none -> 13 us  [the longest x1 8.21 us: per_device(): gathered = lax.all_to_all(pieces, 'inst', 2, 0, tiled=False)]
    broadcast_in_dim x0 -> x1, other arithmetic: none -> 10.1 us  [per_device(): return (derivative.reshape(induced.shape) - induced)[None]]
    sub x2 -> x0, other arithmetic: 8.48 us -> none  [the longest x1 8.43 us: per_device(): return derivative - induced]
    another operation x0 -> x1, local copies, waits for them, and re-layouts: none -> 3.97 us  [per_device(): gathered = lax.all_to_all(pieces, 'inst', 2, 0, tiled=False)]
    broadcast_in_dim x0 -> x1, local copies, waits for them, and re-layouts: none -> 3.49 us  [per_device(): derivative = lax.all_to_all(mixed, 'inst', 0, 2, tiled=False)]
  transfers between devices with their start and end apart: 3 -> 4, of which waited for: 1 -> 2; matrix products, arithmetic and copies ran while one was open for 11% -> 40% of each run, Pallas kernels for 0% -> 0%
where the time goes in v1:
time: 114 us; the launch traced here: 113 us
  waiting for transfers between devices  38.7 us (34%)
  other arithmetic  27.3 us (24%)
  local copies, waits for them, and re-layouts  26.6 us (23%)
  starting transfers between devices  13.5 us (12%)
  matrix products  6.33 us (6%)
    all_to_all x1, waiting for transfers between devices, per_device(): gathered = lax.all_to_all(pieces, 'inst', 2, 0, tiled=False)  21.5 us
    all_to_all x1, waiting for transfers between devices, per_device(): derivative = lax.all_to_all(mixed, 'inst', 0, 2, tiled=False)  17.1 us
    broadcast_in_dim x1, other arithmetic, per_device(): return (derivative.reshape(induced.shape) - induced)[None]  10.1 us
    concatenate x8, local copies, waits for them, and re-layouts, deriv_axis(): return (jnp.roll(values, -1, axis) - jnp.roll(values, 1, axis)) * 0.5  9.41 us
    slice x4, local copies, waits for them, and re-layouts, second_axis(): return jnp.roll(values, -1, axis) + jnp.roll(values, 1, axis) - 2.0 * values  9.01 us
    all_to_all x1, starting transfers between devices, per_device(): gathered = lax.all_to_all(pieces, 'inst', 2, 0, tiled=False)  8.21 us
    dot_general x1, matrix products, per_device(): jnp.einsum('nm,mczxy->nczxy', matrix, gathered, precision=lax.Precision.H...  6.33 us
    sub x1, other arithmetic, induction(): deriv_axis(emf_x, 0) - x_deriv[2]  4.76 us
  transfers between devices with their start and end apart: 4, of which 2 were waited for; matrix products, arithmetic and copies ran while one was open for 40% of the time, Pallas kernels for 0%

profile of v1, /device:TPU:2, one launch (start us, length us, event | category | flops | bytes accessed | tf_op | source)
XLA Modules:
  0.0 112.7 jit_solution(5440821327590422596)
XLA Ops:
  0.0 4.0 %copy.13 = f32[1,3,4,8,8,1024]{5,4,2,1,0,3:T(8,128)} copy(f32[1,3,4,8,8,1024]{5,4,3,2,1,0:T(8,128)} %bitcast.63) | data formatting | bytes 6291456 | tf_op jit(solution)/shard_map/broadcast_in_dim;reshape;squeeze | solution.py:77
  4.0 0.0 copy-start
  4.0 8.2 %all-to-all-start = ((f32[1,3,4,8,8,1024]{5,4,2,1,0,3:T(8,128)}), f32[1,3,4,8,8,1024]{5,4,2,1,0,3:T(8,128)}, u32[]{:S(2)}, u32[]{:S(2)}) async-start(f32[1,3,4,8,8,1024]{5,4,2,1,0,3:T(8,128)} %copy.13), calls=%async_computation | async-start | bytes 6291456 | tf_op jit(solution)/shard_map/all_to_all | solution.py:77
  12.2 0.0 copy-done
  12.2 2.9 %multiply_subtract_fusion.1 = (f32[1,1,4,64,1024]{4,3,2,1,0:T(8,128)S(1)}, f32[1,1,4,64,1024]{4,3,2,1,0:T(8,128)S(1)}, f32[1,1,4,64,1024]{4,3,2,1,0:T(8,128)S(1)}) fusion(f32[1,3,4,64,1024]{4,3,2,1,0:T(8,128)S(1)} %copy-done, f32[1,3,4,64,1024]{4,3,2,1,0:T(8,128)} %param.3), kind=kLoop, calls=%fused_computation.35 | loop fusion | flops 2359296 | bytes 9437184 | tf_op jit(solution)/shard_map/sub | solution.py:50
  15.1 0.0 copy-start.5
  15.1 0.0 copy-start.1
  15.1 0.0 copy-start.3
  15.1 1.1 pad_maximum_fusion.4
  16.2 0.0 collective-permute-start
  16.2 0.5 collective-permute-start.1
  16.7 0.8 slice_bitcast_fusion.12
  17.5 0.8 slice_bitcast_fusion.14
  18.2 0.9 slice_bitcast_fusion.8
  19.1 0.8 slice_bitcast_fusion.10
  20.0 0.9 fusion.64
  20.8 1.3 %slice_bitcast_fusion.4 = (f32[1,3,64,1024]{3,2,1,0:T(8,128)}, f32[1,3,64,1024]{3,2,1,0:T(8,128)}) fusion(f32[1,1,4,64,1024]{4,3,2,1,0:T(8,128)S(1)} %get-tuple-element.11), kind=kLoop, calls=%fused_computation.38 | loop fusion | bytes 3145728 | tf_op jit(solution)/shard_map/jit(_roll_static)/concatenate | solution.py:42
  22.2 0.0 copy-done.5
  22.2 1.4 %slice_bitcast_fusion.6 = (f32[1,3,64,1024]{3,2,1,0:T(8,128)}, f32[1,3,64,1024]{3,2,1,0:T(8,128)}) fusion(f32[1,1,4,64,1024]{4,3,2,1,0:T(8,128)S(1)} %get-tuple-element.13), kind=kLoop, calls=%fused_computation.40 | loop fusion | bytes 3145728 | tf_op jit(solution)/shard_map/jit(_roll_static)/concatenate | solution.py:42
  23.5 1.4 %fusion.66 = (f32[3,1,64,1024]{3,2,1,0:T(8,128)}, f32[3,1,64,1024]{3,2,1,0:T(8,128)}) fusion(f32[3,4,64,1024]{3,2,1,0:T(8,128)S(1)} %bitcast.66), kind=kLoop, calls=%fused_computation.102 | loop fusion | bytes 3145728 | tf_op jit(solution)/shard_map/jit(_roll_static)/slice | solution.py:46
  24.9 0.0 copy-done.1
  24.9 1.8 %slice_bitcast_fusion = (f32[1,4,64,1023]{3,2,1,0:T(8,128)}, f32[1,4,64,1023]{3,2,1,0:T(8,128)}) fusion(f32[4,64,1024]{2,1,0:T(8,128)S(1)} %bitcast.73), kind=kLoop, calls=%fused_computation.20 | loop fusion | bytes 4190208 | tf_op jit(solution)/shard_map/jit(_roll_static)/concatenate | solution.py:42
  26.7 0.0 copy-done.3
  26.7 1.7 %slice_bitcast_fusion.2 = (f32[1,4,64,1023]{3,2,1,0:T(8,128)}, f32[1,4,64,1023]{3,2,1,0:T(8,128)}) fusion(f32[4,64,1024]{2,1,0:T(8,128)S(1)} %bitcast.78), kind=kLoop, calls=%fused_computation.24 | loop fusion | bytes 4190208 | tf_op jit(solution)/shard_map/jit(_roll_static)/concatenate | solution.py:42
  28.4 21.5 %all-to-all-done = f32[1,3,4,8,8,1024]{5,4,2,1,0,3:T(8,128)} async-done(((f32[1,3,4,8,8,1024]{5,4,2,1,0,3:T(8,128)}), f32[1,3,4,8,8,1024]{5,4,2,1,0,3:T(8,128)}, u32[]{:S(2)}, u32[]{:S(2)}) %all-to-all-start) | async-done | bytes 3145760 | tf_op jit(solution)/shard_map/all_to_all | solution.py:77
  49.9 6.3 %fusion.12 = f32[8,3,4,1,8,1024]{5,0,4,2,1,3:T(8,128)S(1)} fusion(f32[1,3,4,8,8,1024]{5,4,2,1,0,3:T(8,128)} %all-to-all-done), kind=kOutput, calls=%fused_computation.19 | convolution fusion | flops 75499392 | bytes 6291456 | tf_op jit(solution)/shard_map/nm,mczxy->nczxy/dot_general | solution.py:78
  56.3 3.5 %copy.15 = f32[8,3,4,1,8,1024]{5,4,2,1,3,0:T(8,128)} copy(f32[8,3,4,1,8,1024]{5,0,4,2,1,3:T(8,128)S(1)} %fusion.12) | data formatting | bytes 6291456 | tf_op jit(solution)/shard_map/broadcast_in_dim | solution.py:79
  59.8 4.8 %all-to-all-start.1 = ((f32[8,3,4,1,8,1024]{5,4,2,1,3,0:T(8,128)}), f32[8,3,4,1,8,1024]{5,4,2,1,3,0:T(8,128)}, u32[]{:S(2)}, u32[]{:S(2)}) async-start(f32[8,3,4,1,8,1024]{5,4,2,1,3,0:T(8,128)} %copy.15), calls=%async_computation.1 | async-start | bytes 6291456 | tf_op jit(solution)/shard_map/all_to_all | solution.py:79
  64.5 2.9 %fusion.67 = (f32[3,3,64,1024]{3,2,1,0:T(8,128)}, f32[3,3,64,1024]{3,2,1,0:T(8,128)}) fusion(f32[3,4,64,1024]{3,2,1,0:T(8,128)S(1)} %bitcast.67), kind=kLoop, calls=%fused_computation.103 | loop fusion | bytes 9437184 | tf_op jit(solution)/shard_map/jit(_roll_static)/slice | solution.py:46
  67.4 0.0 copy-start.7
  67.4 0.0 copy-start.8
  67.4 0.0 copy-start.9
  67.4 0.0 copy-start.10
  67.4 0.0 copy-start.11
  67.4 0.0 copy-start.12
  67.4 0.0 copy-start.13
  67.4 0.0 copy-start.14
  67.4 3.9 %fusion.65 = (f32[3,4,64,1023]{3,2,1,0:T(8,128)}, f32[3,4,64,1023]{3,2,1,0:T(8,128)}) fusion(f32[3,4,64,1024]{3,2,1,0:T(8,128)S(1)} %bitcast.68), kind=kLoop, calls=%fused_computation.101 | loop fusion | bytes 12570624 | tf_op jit(solution)/shard_map/jit(_roll_static)/slice | solution.py:46
  71.3 0.0 copy-start.2
  71.4 0.0 copy-start.4
  71.4 0.0 copy-start.6
  71.4 0.0 copy-done.7
  71.4 0.0 copy-done.8
  71.4 0.0 copy-done.9
  71.4 0.0 copy-done.10
  71.4 0.0 copy-done.11
  71.4 0.0 copy-done.12
  71.4 0.0 copy-done.13
  71.4 0.0 copy-done.14
  71.4 1.4 %fusion.16 = f32[1,4,64,1024]{3,2,1,0:T(8,128)} fusion(f32[1,4,64,1]{3,2,1,0:T(8,128)S(1)} %copy-done.14, f32[1,4,64,1023]{3,2,1,0:T(8,128)S(1)} %copy-done.8, f32[1,4,64,1023]{3,2,1,0:T(8,128)S(1)} %copy-done.7, f32[1,4,64,1]{3,2,1,0:T(8,128)S(1)} %copy-done.13, f32[1,1,64,1024]{3,2,1,0:T(8,128)S(1)} %copy-done.12, f32[1,3,64,1024]{3,2,1,0:T(8,128)S(1)} %copy-done.10, ...), kind=kLoop, calls=%fused_computation.28 | loop fusion | flops 2359296 | bytes 5242880 | tf_op jit(solution)/shard_map/sub | solution.py:60
  72.9 0.0 collective-permute-done
  72.9 0.0 collective-permute-done.1
  72.9 0.0 copy-done.2
  72.9 0.2 copy-done.4
  73.0 0.6 copy-done.6
  73.6 2.7 %pad_maximum_fusion = (f32[6,4,65,1024]{3,2,1,0:T(8,128)S(1)}, f32[6,4,65,1024]{3,2,1,0:T(8,128)S(1)}) fusion(f32[6,4,1,1024]{3,2,1,0:T(1,128)} %collective-permute-done, f32[3,4,64,1024]{3,2,1,0:T(8,128)S(1)} %bitcast.69, f32[1,4,64,1024]{3,2,1,0:T(8,128)S(1)} %bitcast.80, f32[1,4,64,1024]{3,2,1,0:T(8,128)S(1)} %bitcast.83, ...), kind=kLoop, calls=%fused_computation | loop fusion | flops 12779520 | bytes 19267584 | tf_op jit(solution)/shard_map/concatenate | solution.py:15
  76.3 4.3 %fusion = f32[6,4,64,1024]{3,2,1,0:T(8,128)} fusion(f32[6,4,65,1024]{3,2,1,0:T(8,128)S(1)} %get-tuple-element.8, f32[6,4,65,1024]{3,2,1,0:T(8,128)S(1)} %get-tuple-element.7), kind=kLoop, calls=%fused_computation.3 | loop fusion | flops 3145728 | bytes 18874368 | tf_op jit(solution)/shard_map/mul | solution.py:57
  80.6 4.8 %slice_subtract_fusion.2 = (f32[1,4,64,1024]{3,2,1,0:T(8,128)}, f32[1,4,64,1024]{3,2,1,0:T(8,128)}) fusion(f32[6,4,64,1024]{3,2,1,0:T(8,128)} %fusion, f32[1,1,64,1024]{3,2,1,0:T(8,128)} %get-tuple-element.31, f32[1,3,64,1024]{3,2,1,0:T(8,128)} %get-tuple-element.33, f32[1,3,64,1024]{3,2,1,0:T(8,128)} %get-tuple-element.32, ...), kind=kLoop, calls=%fused_computation.23 | loop fusion | flops 2621440 | bytes 8388608 | tf_op jit(solution)/shard_map/sub | solution.py:61
  85.3 17.1 %all-to-all-done.1 = f32[8,3,4,1,8,1024]{5,4,2,1,3,0:T(8,128)} async-done(((f32[8,3,4,1,8,1024]{5,4,2,1,3,0:T(8,128)}), f32[8,3,4,1,8,1024]{5,4,2,1,3,0:T(8,128)}, u32[]{:S(2)}, u32[]{:S(2)}) %all-to-all-start.1) | async-done | bytes 3145760 | tf_op jit(solution)/shard_map/all_to_all | solution.py:79
  102.5 10.1 %fusion.7 = f32[1,3,4,64,1024]{4,3,2,1,0:T(8,128)} fusion(f32[6,4,1,1024]{3,2,1,0:T(1,128)} %collective-permute-done.1, f32[3,4,64,1024]{3,2,1,0:T(8,128)S(1)} %bitcast.70, f32[1,4,64,1024]{3,2,1,0:T(8,128)} %bitcast.79, f32[1,4,64,1024]{3,2,1,0:T(8,128)} %bitcast.82, f32[1,4,64,1024]{3,2,1,0:T(8,128)} %bitcast.74, ...), kind=kLoop, calls=%fused_computation.11 | loop fusion | flops 20447232 | bytes 28508160 | tf_op jit(solution)/shard_map/broadcast_in_dim | solution.py:80
Async XLA Ops:
  4.0 8.2 %copy-start = (f32[1,3,4,64,1024]{4,3,2,1,0:T(8,128)S(1)}, f32[1,3,4,64,1024]{4,3,2,1,0:T(8,128)}, u32[]{:S(2)}) copy-start(f32[1,3,4,64,1024]{4,3,2,1,0:T(8,128)} %param.2) | copy-start | bytes 9437188
  4.0 46.0 %all-to-all-start = ((f32[1,3,4,8,8,1024]{5,4,2,1,0,3:T(8,128)}), f32[1,3,4,8,8,1024]{5,4,2,1,0,3:T(8,128)}, u32[]{:S(2)}, u32[]{:S(2)}) async-start(f32[1,3,4,8,8,1024]{5,4,2,1,0,3:T(8,128)} %copy.13), calls=%async_computation | async-start | bytes 6291456 | tf_op jit(solution)/shard_map/all_to_all | solution.py:77
  15.1 7.1 %copy-start.5 = (f32[1,1,4,64,1024]{4,3,2,1,0:T(8,128)}, f32[1,1,4,64,1024]{4,3,2,1,0:T(8,128)S(1)}, u32[]{:S(2)}) copy-start(f32[1,1,4,64,1024]{4,3,2,1,0:T(8,128)S(1)} %get-tuple-element.13) | copy-start | bytes 3145732
  15.1 9.8 %copy-start.1 = (f32[1,1,4,64,1024]{4,3,2,1,0:T(8,128)}, f32[1,1,4,64,1024]{4,3,2,1,0:T(8,128)S(1)}, u32[]{:S(2)}) copy-start(f32[1,1,4,64,1024]{4,3,2,1,0:T(8,128)S(1)} %get-tuple-element.11) | copy-start | bytes 3145732
  15.1 11.5 %copy-start.3 = (f32[1,1,4,64,1024]{4,3,2,1,0:T(8,128)}, f32[1,1,4,64,1024]{4,3,2,1,0:T(8,128)S(1)}, u32[]{:S(2)}) copy-start(f32[1,1,4,64,1024]{4,3,2,1,0:T(8,128)S(1)} %get-tuple-element.12) | copy-start | bytes 3145732
  16.2 56.6 %collective-permute-start = (f32[6,4,1,1024]{3,2,1,0:T(1,128)}, f32[6,4,1,1024]{3,2,1,0:T(1,128)}, u32[]{:S(2)}, u32[]{:S(2)}) collective-permute-start(f32[6,4,1,1024]{3,2,1,0:T(1,128)} %get-tuple-element.9), channel_id=1, source_target_pairs={{1,0},{2,1},{3,2},{4,3},{5,4},{6,5},{7,6},{8,7},{9,8},{10,9},{11,1... | collective-permute-start | bytes 294920 | tf_op jit(solution)/shard_map/ppermute | solution.py:19
  16.2 56.6 %collective-permute-start.1 = (f32[6,4,1,1024]{3,2,1,0:T(1,128)}, f32[6,4,1,1024]{3,2,1,0:T(1,128)}, u32[]{:S(2)}, u32[]{:S(2)}) collective-permute-start(f32[6,4,1,1024]{3,2,1,0:T(1,128)} %get-tuple-element.10), channel_id=1, source_target_pairs={{0,1},{1,2},{2,3},{3,4},{4,5},{5,6},{6,7},{7,8},{8,9},{9,10},{10,1... | collective-permute-start | bytes 294920 | tf_op jit(solution)/shard_map/ppermute | solution.py:17
  59.8 42.7 %all-to-all-start.1 = ((f32[8,3,4,1,8,1024]{5,4,2,1,3,0:T(8,128)}), f32[8,3,4,1,8,1024]{5,4,2,1,3,0:T(8,128)}, u32[]{:S(2)}, u32[]{:S(2)}) async-start(f32[8,3,4,1,8,1024]{5,4,2,1,3,0:T(8,128)} %copy.15), calls=%async_computation.1 | async-start | bytes 6291456 | tf_op jit(solution)/shard_map/all_to_all | solution.py:79
  67.4 4.0 %copy-start.7 = (f32[1,4,64,1023]{3,2,1,0:T(8,128)S(1)}, f32[1,4,64,1023]{3,2,1,0:T(8,128)}, u32[]{:S(2)}) copy-start(f32[1,4,64,1023]{3,2,1,0:T(8,128)} %get-tuple-element.28) | copy-start | bytes 3142660
  67.4 4.0 %copy-start.8 = (f32[1,4,64,1023]{3,2,1,0:T(8,128)S(1)}, f32[1,4,64,1023]{3,2,1,0:T(8,128)}, u32[]{:S(2)}) copy-start(f32[1,4,64,1023]{3,2,1,0:T(8,128)} %get-tuple-element.29) | copy-start | bytes 3142660
  67.4 4.0 %copy-start.9 = (f32[1,3,64,1024]{3,2,1,0:T(8,128)S(1)}, f32[1,3,64,1024]{3,2,1,0:T(8,128)}, u32[]{:S(2)}) copy-start(f32[1,3,64,1024]{3,2,1,0:T(8,128)} %get-tuple-element.24) | copy-start | bytes 2359300
  67.4 4.0 %copy-start.10 = (f32[1,3,64,1024]{3,2,1,0:T(8,128)S(1)}, f32[1,3,64,1024]{3,2,1,0:T(8,128)}, u32[]{:S(2)}) copy-start(f32[1,3,64,1024]{3,2,1,0:T(8,128)} %get-tuple-element.25) | copy-start | bytes 2359300
  67.4 4.0 %copy-start.11 = (f32[1,1,64,1024]{3,2,1,0:T(8,128)S(1)}, f32[1,1,64,1024]{3,2,1,0:T(8,128)}, u32[]{:S(2)}) copy-start(f32[1,1,64,1024]{3,2,1,0:T(8,128)} %get-tuple-element.22) | copy-start | bytes 786436
  67.4 4.0 %copy-start.12 = (f32[1,1,64,1024]{3,2,1,0:T(8,128)S(1)}, f32[1,1,64,1024]{3,2,1,0:T(8,128)}, u32[]{:S(2)}) copy-start(f32[1,1,64,1024]{3,2,1,0:T(8,128)} %get-tuple-element.23) | copy-start | bytes 786436
  67.4 4.0 %copy-start.13 = (f32[1,4,64,1]{3,2,1,0:T(8,128)S(1)}, f32[1,4,64,1]{3,2,1,0:T(8,128)}, u32[]{:S(2)}) copy-start(f32[1,4,64,1]{3,2,1,0:T(8,128)} %get-tuple-element.26) | copy-start | bytes 3076
  67.4 4.0 %copy-start.14 = (f32[1,4,64,1]{3,2,1,0:T(8,128)S(1)}, f32[1,4,64,1]{3,2,1,0:T(8,128)}, u32[]{:S(2)}) copy-start(f32[1,4,64,1]{3,2,1,0:T(8,128)} %get-tuple-element.27) | copy-start | bytes 3076
  71.3 1.5 %copy-start.2 = (f32[1,1,4,64,1024]{4,3,2,1,0:T(8,128)S(1)}, f32[1,1,4,64,1024]{4,3,2,1,0:T(8,128)}, u32[]{:S(2)}) copy-start(f32[1,1,4,64,1024]{4,3,2,1,0:T(8,128)} %copy-done.1) | copy-start | bytes 3145732
  71.4 1.7 %copy-start.4 = (f32[1,1,4,64,1024]{4,3,2,1,0:T(8,128)S(1)}, f32[1,1,4,64,1024]{4,3,2,1,0:T(8,128)}, u32[]{:S(2)}) copy-start(f32[1,1,4,64,1024]{4,3,2,1,0:T(8,128)} %copy-done.3) | copy-start | bytes 3145732
  71.4 2.2 %copy-start.6 = (f32[1,1,4,64,1024]{4,3,2,1,0:T(8,128)S(1)}, f32[1,1,4,64,1024]{4,3,2,1,0:T(8,128)}, u32[]{:S(2)}) copy-start(f32[1,1,4,64,1024]{4,3,2,1,0:T(8,128)} %copy-done.5) | copy-start | bytes 3145732

commit v2 on v1

v2 whole, which is shorter than its diff:
```python
import functools

import jax
import jax.numpy as jnp
import numpy as np
from jax import lax
from jax.experimental import pallas as pl
from jax.experimental.pallas import tpu as pltpu
from jax.sharding import PartitionSpec as P

RESIST = 0.2
TIME_DAMP = 0.5
LANES = 256
MESH = pl.DeviceIdType.MESH


def time_weights(count):
    k = np.arange(1, count)
    parity = np.where(k % 2 == 0, 1.0, -1.0)
    sine, cosine = np.sin(np.pi * k / count), np.cos(np.pi * k / count)
    off = 0.5 * parity * cosine / sine + TIME_DAMP * 0.5 * parity / (sine * sine)
    return [TIME_DAMP * (count * count + 2) / 12.0] + [float(v) for v in off]


def mix(fields, weights):
    count = len(fields)
    half = count // 2
    sums = [fields[k] + fields[k + half] for k in range(half)]
    diffs = [fields[k] - fields[k + half] for k in range(half)]

    def dot(terms, row):
        total = None
        for term, weight in zip(terms, row):
            part = term * np.float32(weight)
            total = part if total is None else total + part
        return total

    low, high = [], []
    for q in range(half):
        row = [weights[(q + k) % count] for k in range(half)]
        far = [weights[(q + k + half) % count] for k in range(half)]
        even = dot(sums, [(a + b) / 2 for a, b in zip(row, far)])
        odd = dot(diffs, [(a - b) / 2 for a, b in zip(row, far)])
        low.append(even + odd)
        high.append(even - odd)
    return low + high


def cross(u, b):
    return [u[1] * b[2] - u[2] * b[1], u[2] * b[0] - u[0] * b[2], u[0] * b[1] - u[1] * b[0]]


def x_terms(b, e, sign):
    half = np.float32(0.5 * sign)
    rate = np.float32(RESIST)
    return [rate * b[0], rate * b[1] - half * e[2], rate * b[2] + half * e[1]]


def kernel(weights, b_hbm, u_hbm, mixed, induced, field, flow, emf, got, out, edge, halo,
           load_sem, edge_send, edge_recv, there_send, there_recv, back_send, back_recv):
    count = len(weights)
    comps, planes, rows, lanes = field.shape
    part = rows // count
    me, tile = lax.axis_index("inst"), lax.axis_index("tile")
    tiles = lax.axis_size("tile")
    peers = [lax.rem(me + k, count) for k in range(count)]
    after, before = lax.rem(tile + 1, tiles), lax.rem(tile + tiles - 1, tiles)

    barrier = pltpu.get_barrier_semaphore()
    for k in range(1, count):
        pl.semaphore_signal(barrier, inc=1, device_id=(peers[k], tile), device_id_type=MESH)
    for other in (before, after):
        pl.semaphore_signal(barrier, inc=1, device_id=(me, other), device_id_type=MESH)

    loads = [pltpu.make_async_copy(b_hbm, field, load_sem.at[0]), pltpu.make_async_copy(u_hbm, flow, load_sem.at[1])]
    for load in loads:
        load.start()
    for load in loads:
        load.wait()

    for side, (first, row, sign) in enumerate(((0, 0, 1), (rows - 8, 7, -1))):
        for z in range(planes):
            b = [field[c, z, first:first + 8, :] for c in range(comps)]
            e = cross([flow[c, z, first:first + 8, :] for c in range(comps)], b)
            for c, term in enumerate(x_terms(b, e, sign)):
                at = c * planes + z
                edge[side, at:at + 1, :] = term[row:row + 1, :]

    pl.semaphore_wait(barrier, count + 1)

    def edge_copy(side, other):
        return pltpu.make_async_remote_copy(
            src_ref=edge.at[side], dst_ref=halo.at[side], send_sem=edge_send.at[side], recv_sem=edge_recv.at[side],
            device_id=(me, other), device_id_type=MESH)

    edges = [edge_copy(0, before), edge_copy(1, after)]
    for copy in edges:
        copy.start()

    def there(z, k):
        return pltpu.make_async_remote_copy(
            src_ref=field.at[:, z, pl.ds(pl.multiple_of(peers[k] * part, part), part), :], dst_ref=got.at[k - 1, z],
            send_sem=there_send.at[z, k - 1], recv_sem=there_recv.at[z, k - 1],
            device_id=(peers[k], tile), device_id_type=MESH)

    own = pl.ds(pl.multiple_of(me * part, part), part)

    def back(z, k):
        return pltpu.make_async_remote_copy(
            src_ref=out.at[k - 1, z], dst_ref=mixed.at[:, z, own, :],
            send_sem=back_send.at[z, k - 1], recv_sem=back_recv.at[z, k - 1],
            device_id=(peers[k], tile), device_id_type=MESH)

    for z in range(planes):
        for k in range(1, count):
            there(z, k).start()

    def emf_plane(z, carry):
        b = [field[c, z] for c in range(comps)]
        for c, value in enumerate(cross([flow[c, z] for c in range(comps)], b)):
            emf[c, z] = value
        return carry

    lax.fori_loop(0, planes, emf_plane, 0)

    for copy in edges:
        copy.wait()

    rate, half = np.float32(RESIST), np.float32(0.5)

    def induction_plane(z, carry):
        up, down = lax.rem(z + 1, planes), lax.rem(z + planes - 1, planes)
        b = [field[c, z] for c in range(comps)]
        e = [emf[c, z] for c in range(comps)]
        place = lax.broadcasted_iota(jnp.int32, (rows, lanes), 0)
        from_after, from_before = x_terms(b, e, 1), x_terms(b, e, -1)
        z_emf = [lambda at: -emf[1, at], lambda at: emf[0, at], lambda at: None]
        y_emf = [e[2], None, -e[0]]
        for c in range(comps):
            total = np.float32(-6.0 * RESIST) * b[c]
            total += rate * (field[c, up] + field[c, down])
            if c < 2:
                total += half * (z_emf[c](up) - z_emf[c](down))
            diffusive = rate * b[c]
            ahead, behind = diffusive, diffusive
            if y_emf[c] is not None:
                ahead, behind = diffusive + half * y_emf[c], diffusive - half * y_emf[c]
            total += pltpu.roll(ahead, lanes - 1, 1) + pltpu.roll(behind, 1, 1)
            row = c * planes + z
            next_row, last_row = halo[0, pl.ds(row, 1), :], halo[1, pl.ds(row, 1), :]
            total += jnp.where(place == rows - 1, next_row, pltpu.roll(from_after[c], rows - 1, 0))
            total += jnp.where(place == 0, last_row, pltpu.roll(from_before[c], 1, 0))
            induced[c, z] = total
        return carry

    lax.fori_loop(0, planes, induction_plane, 0)

    steps = lanes // LANES
    for z in range(planes):
        for k in range(1, count):
            there(z, k).wait_recv()

        def mix_block(i, carry, z=z):
            c, at = i // steps, pl.ds(pl.multiple_of((i % steps) * LANES, LANES), LANES)
            fields = [field[c, z, own, at]] + [got[k, z, c, :, at] for k in range(count - 1)]
            values = mix(fields, weights)
            mixed[c, z, own, at] = values[0]
            for k in range(1, count):
                out[k - 1, z, c, :, at] = values[k]
            return carry

        lax.fori_loop(0, comps * steps, mix_block, 0)
        for k in range(1, count):
            back(z, k).start()

    for z in range(planes):
        for k in range(1, count):
            there(z, k).wait_send()
            back(z, k).wait()


def per_device(magnetic, velocity):
    inst_count = lax.axis_size("inst")
    field, flow = (pltpu.with_memory_space_constraint(a[0], pltpu.HBM) for a in (magnetic, velocity))
    shape = field.shape
    comps, planes, rows, lanes = shape
    part = rows // inst_count
    vmem = pl.BlockSpec(memory_space=pltpu.VMEM)
    block = jax.ShapeDtypeStruct(shape, jnp.float32)
    mixed, induced = pl.pallas_call(
        functools.partial(kernel, time_weights(inst_count)),
        out_shape=(block, block),
        in_specs=[pl.BlockSpec(memory_space=pltpu.HBM)] * 2,
        out_specs=(vmem, vmem),
        scratch_shapes=[
            pltpu.VMEM(shape, jnp.float32),
            pltpu.VMEM(shape, jnp.float32),
            pltpu.VMEM(shape, jnp.float32),
            pltpu.VMEM((inst_count - 1, planes, comps, part, lanes), jnp.float32),
            pltpu.VMEM((inst_count - 1, planes, comps, part, lanes), jnp.float32),
            pltpu.VMEM((2, comps * planes, lanes), jnp.float32),
            pltpu.VMEM((2, comps * planes, lanes), jnp.float32),
            pltpu.SemaphoreType.DMA((2,)),
            pltpu.SemaphoreType.DMA((2,)),
            pltpu.SemaphoreType.DMA((2,)),
            pltpu.SemaphoreType.DMA((planes, inst_count - 1)),
            pltpu.SemaphoreType.DMA((planes, inst_count - 1)),
            pltpu.SemaphoreType.DMA((planes, inst_count - 1)),
            pltpu.SemaphoreType.DMA((planes, inst_count - 1)),
        ],
        compiler_params=pltpu.CompilerParams(
            collective_id=0, has_side_effects=True, vmem_limit_bytes=40 * 2**20
        ),
    )(field, flow)
    return (mixed - induced)[None]


def solution(mesh):
    in_specs = (P("inst", None, None, "tile", None), P("inst", None, None, "tile", None))
    out_specs = P("inst", None, None, "tile", None)
    return jax.shard_map(
        per_device, mesh=mesh, in_specs=in_specs, out_specs=out_specs, check_vma=False
    )
```

time: 114 us -> 82.5 us (0.72); the launches traced: 113 us -> 82.4 us
  Pallas kernels: 0 us -> 79.8 us
  waiting for transfers between devices: 38.7 us -> 0 us
  local copies, waits for them, and re-layouts: 26.6 us -> 0 us
  other arithmetic: 27.3 us -> 2.63 us
  starting transfers between devices: 13.5 us -> 0 us
  matrix products: 6.33 us -> 0 us
    pallas_call x0 -> x1, Pallas kernels: none -> 79.8 us  [per_device(): pl.pallas_call(functools.partial(kernel, time_weights(inst_count)), out_s...]
    all_to_all x2 -> x0, waiting for transfers between devices: 38.7 us -> none  [the longest x1 21.5 us: per_device(): gathered = lax.all_to_all(pieces, 'inst', 2, 0, tiled=False)]
    all_to_all x2 -> x0, starting transfers between devices: 13 us -> none  [the longest x1 8.21 us: per_device(): gathered = lax.all_to_all(pieces, 'inst', 2, 0, tiled=False)]
    concatenate x8 -> x0, local copies, waits for them, and re-layouts: 9.41 us -> none  [deriv_axis(): return (jnp.roll(values, -1, axis) - jnp.roll(values, 1, axis)) * 0.5]
    sub x3 -> x0, other arithmetic: 9.09 us -> none  [the longest x1 4.76 us: induction(): deriv_axis(emf_x, 0) - x_deriv[2]]
    slice x4 -> x0, local copies, waits for them, and re-layouts: 9.01 us -> none  [second_axis(): return jnp.roll(values, -1, axis) + jnp.roll(values, 1, axis) - 2.0 * values]
    broadcast_in_dim x1, other arithmetic: 10.1 us -> 2.63 us  [per_device(): return (mixed - induced)[None]]
    dot_general x1 -> x0, matrix products: 6.33 us -> none  [per_device(): jnp.einsum('nm,mczxy->nczxy', matrix, gathered, precision=lax.Precision.H...]
  transfers between devices with their start and end apart: 4 -> 0, of which waited for: 2 -> 0; matrix products, arithmetic and copies ran while one was open for 40% -> 0% of each run, Pallas kernels for 0% -> 0%
where the time goes in v2:
time: 82.5 us; the launch traced here: 82.4 us
  Pallas kernels  79.8 us (97%)
  other arithmetic  2.63 us (3%)
    pallas_call x1, Pallas kernels, per_device(): pl.pallas_call(functools.partial(kernel, time_weights(inst_count)), out_s...  79.8 us
    broadcast_in_dim x1, other arithmetic, per_device(): return (mixed - induced)[None]  2.63 us

profile of v2, /device:TPU:2, one launch (start us, length us, event | category | flops | bytes accessed | tf_op | source)
XLA Modules:
  0.0 82.4 jit_solution(9957398874204966421)
XLA Ops:
  0.0 79.8 %shard_map.28 = (f32[3,4,64,1024]{3,2,1,0:T(8,128)S(1)}, f32[3,4,64,1024]{3,2,1,0:T(8,128)S(1)}) custom-call(f32[3,4,64,1024]{3,2,1,0:T(8,128)} %bitcast.4, f32[3,4,64,1024]{3,2,1,0:T(8,128)} %bitcast.5), custom_call_target="tpu_custom_call" | custom-call | tf_op jit(solution)/shard_map/pallas_call | solution.py:190
  79.8 2.6 %subtract_bitcast_fusion = f32[1,3,4,64,1024]{4,3,2,1,0:T(8,128)} fusion(f32[3,4,64,1024]{3,2,1,0:T(8,128)S(1)} %get-tuple-element.7, f32[3,4,64,1024]{3,2,1,0:T(8,128)S(1)} %get-tuple-element.8), kind=kLoop, calls=%fused_computation | loop fusion | flops 786432 | bytes 9437184 | tf_op jit(solution)/shard_map/broadcast_in_dim | solution.py:215

commit v3 on v2

--- a/solution.py
+++ b/solution.py
@@ -11,6 +11,11 @@
 RESIST = 0.2
 TIME_DAMP = 0.5
 LANES = 256
+RING = 4
+NEAR = ((0, 1), (0, -1), (0, 2), (1, 0))
+FAR = ((1, 1), (1, -1), (1, 2))
+STEPS = NEAR + FAR
+ACROSS = (1, 0)
 MESH = pl.DeviceIdType.MESH
 
 
@@ -57,24 +62,60 @@
 
 
 def kernel(weights, b_hbm, u_hbm, mixed, induced, field, flow, emf, got, out, edge, halo,
-           load_sem, edge_send, edge_recv, there_send, there_recv, back_send, back_recv):
+           load_sem, edge_send, edge_recv, there_send, there_recv, back_send, back_recv, ready):
     count = len(weights)
     comps, planes, rows, lanes = field.shape
     part = rows // count
     me, tile = lax.axis_index("inst"), lax.axis_index("tile")
     tiles = lax.axis_size("tile")
-    peers = [lax.rem(me + k, count) for k in range(count)]
     after, before = lax.rem(tile + 1, tiles), lax.rem(tile + tiles - 1, tiles)
 
+    def moved(step):
+        return lax.rem(me // RING + step[0], 2) * RING + lax.rem(me % RING + step[1] + RING, RING)
+
+    def slot(step):
+        return lax.rem(moved(step) - me + count, count) - 1
+
     barrier = pltpu.get_barrier_semaphore()
-    for k in range(1, count):
-        pl.semaphore_signal(barrier, inc=1, device_id=(peers[k], tile), device_id_type=MESH)
+    for step in NEAR:
+        pl.semaphore_signal(barrier, inc=1, device_id=(moved(step), tile), device_id_type=MESH)
     for other in (before, after):
         pl.semaphore_signal(barrier, inc=1, device_id=(me, other), device_id_type=MESH)
 
     loads = [pltpu.make_async_copy(b_hbm, field, load_sem.at[0]), pltpu.make_async_copy(u_hbm, flow, load_sem.at[1])]
     for load in loads:
         load.start()
+    pl.semaphore_wait(barrier, len(NEAR) + 2)
+    pl.semaphore_signal(ready, inc=1, device_id=(moved(ACROSS), tile), device_id_type=MESH)
+
+    def there(z, p):
+        step = STEPS[p]
+        return pltpu.make_async_remote_copy(
+            src_ref=b_hbm.at[:, z, pl.ds(pl.multiple_of(moved(step) * part, part), part), :], dst_ref=got.at[slot(step), z],
+            send_sem=there_send.at[z, p], recv_sem=there_recv.at[z, p],
+            device_id=(moved(step), tile), device_id_type=MESH)
+
+    own = pl.ds(pl.multiple_of(me * part, part), part)
+
+    def back(z, p):
+        step = STEPS[p]
+        return pltpu.make_async_remote_copy(
+            src_ref=out.at[slot(step), z], dst_ref=mixed.at[:, z, own, :],
+            send_sem=back_send.at[z, p], recv_sem=back_recv.at[z, p],
+            device_id=(moved(step), tile), device_id_type=MESH)
+
+    near, far = range(len(NEAR)), range(len(NEAR), len(STEPS))
+    for z in range(2):
+        for p in near:
+            there(z, p).start()
+    pl.semaphore_wait(ready, 1)
+    for z in range(2):
+        for p in far:
+            there(z, p).start()
+    for z in range(2, planes):
+        for p in range(len(STEPS)):
+            there(z, p).start()
+
     for load in loads:
         load.wait()
 
@@ -86,8 +127,6 @@
                 at = c * planes + z
                 edge[side, at:at + 1, :] = term[row:row + 1, :]
 
-    pl.semaphore_wait(barrier, count + 1)
-
     def edge_copy(side, other):
         return pltpu.make_async_remote_copy(
             src_ref=edge.at[side], dst_ref=halo.at[side], send_sem=edge_send.at[side], recv_sem=edge_recv.at[side],
@@ -96,30 +135,30 @@
     edges = [edge_copy(0, before), edge_copy(1, after)]
     for copy in edges:
         copy.start()
-
-    def there(z, k):
-        return pltpu.make_async_remote_copy(
-            src_ref=field.at[:, z, pl.ds(pl.multiple_of(peers[k] * part, part), part), :], dst_ref=got.at[k - 1, z],
-            send_sem=there_send.at[z, k - 1], recv_sem=there_recv.at[z, k - 1],
-            device_id=(peers[k], tile), device_id_type=MESH)
-
-    own = pl.ds(pl.multiple_of(me * part, part), part)
-
-    def back(z, k):
-        return pltpu.make_async_remote_copy(
-            src_ref=out.at[k - 1, z], dst_ref=mixed.at[:, z, own, :],
-            send_sem=back_send.at[z, k - 1], recv_sem=back_recv.at[z, k - 1],
-            device_id=(peers[k], tile), device_id_type=MESH)
-
-    for z in range(planes):
-        for k in range(1, count):
-            there(z, k).start()
 
     def emf_plane(z, carry):
         b = [field[c, z] for c in range(comps)]
         for c, value in enumerate(cross([flow[c, z] for c in range(comps)], b)):
             emf[c, z] = value
         return carry
+
+    steps = lanes // LANES
+    for z in range(planes):
+        for p in range(len(STEPS)):
+            there(z, p).wait_recv()
+
+        def mix_block(i, carry, z=z):
+            c, at = i // steps, pl.ds(pl.multiple_of((i % steps) * LANES, LANES), LANES)
+            fields = [field[c, z, own, at]] + [got[k, z, c, :, at] for k in range(count - 1)]
+            values = mix(fields, weights)
+            mixed[c, z, own, at] = values[0]
+            for k in range(1, count):
+                out[k - 1, z, c, :, at] = values[k]
+            return carry
+
+        lax.fori_loop(0, comps * steps, mix_block, 0)
+        for p in range(len(STEPS)):
+            back(z, p).start()
 
     lax.fori_loop(0, planes, emf_plane, 0)
 
@@ -155,28 +194,19 @@
 
     lax.fori_loop(0, planes, induction_plane, 0)
 
-    steps = lanes // LANES
     for z in range(planes):
-        for k in range(1, count):
-            there(z, k).wait_recv()
-
-        def mix_block(i, carry, z=z):
-            c, at = i // steps, pl.ds(pl.multiple_of((i % steps) * LANES, LANES), LANES)
-            fields = [field[c, z, own, at]] + [got[k, z, c, :, at] for k in range(count - 1)]
-            values = mix(fields, weights)
-            mixed[c, z, own, at] = values[0]
-            for k in range(1, count):
-                out[k - 1, z, c, :, at] = values[k]
-            return carry
-
-        lax.fori_loop(0, comps * steps, mix_block, 0)
-        for k in range(1, count):
-            back(z, k).start()
-
-    for z in range(planes):
-        for k in range(1, count):
-            there(z, k).wait_send()
-            back(z, k).wait()
+        for p in range(len(STEPS)):
+            there(z, p).wait_send()
+            back(z, p).wait()
+
+
+def finish(mixed, induced, result, block, sem):
+    copies = [pltpu.make_async_copy(block.at[i], result.at[i], sem.at[i]) for i in range(block.shape[0])]
+    for i, copy in enumerate(copies):
+        block[i] = mixed[i] - induced[i]
+        copy.start()
+    for copy in copies:
+        copy.wait()
 
 
 def per_device(magnetic, velocity):
@@ -207,12 +237,22 @@
             pltpu.SemaphoreType.DMA((planes, inst_count - 1)),
             pltpu.SemaphoreType.DMA((planes, inst_count - 1)),
             pltpu.SemaphoreType.DMA((planes, inst_count - 1)),
+            pltpu.SemaphoreType.REGULAR,
         ],
         compiler_params=pltpu.CompilerParams(
             collective_id=0, has_side_effects=True, vmem_limit_bytes=40 * 2**20
         ),
     )(field, flow)
-    return (mixed - induced)[None]
+    flat = (comps * planes, rows, lanes)
+    result = pl.pallas_call(
+        finish,
+        out_shape=jax.ShapeDtypeStruct(flat, jnp.float32),
+        in_specs=[vmem, vmem],
+        out_specs=pl.BlockSpec(memory_space=pltpu.HBM),
+        scratch_shapes=[pltpu.VMEM(flat, jnp.float32), pltpu.SemaphoreType.DMA((comps * planes,))],
+        compiler_params=pltpu.CompilerParams(vmem_limit_bytes=40 * 2**20),
+    )(mixed.reshape(flat), induced.reshape(flat))
+    return result.reshape((1,) + shape)
 
 
 def solution(mesh):

time: 82.5 us -> 80.3 us (0.973)
  other arithmetic: 2.63 us -> 0 us
    broadcast_in_dim x1 -> x0, other arithmetic: 2.63 us -> none  [per_device(): return (mixed - induced)[None]]
    pallas_call x1, Pallas kernels: 79.8 us -> 77.7 us  [per_device(): pl.pallas_call(functools.partial(kernel, time_weights(inst_count)), out_s...]
    pallas_call x0 -> x1, Pallas kernels: none -> 1.78 us  [per_device(): pl.pallas_call(finish, out_shape=jax.ShapeDtypeStruct(flat, jnp.float32),...]
where the time goes in v3:
time: 80.3 us; the launch traced here: 79.5 us
  Pallas kernels  79.5 us (99%)
    pallas_call x1, Pallas kernels, per_device(): pl.pallas_call(functools.partial(kernel, time_weights(inst_count)), out_s...  77.7 us
    pallas_call x1, Pallas kernels, per_device(): pl.pallas_call(finish, out_shape=jax.ShapeDtypeStruct(flat, jnp.float32),...  1.78 us

profile of v3, /device:TPU:2, one launch (start us, length us, event | category | flops | bytes accessed | tf_op | source)
XLA Modules:
  0.0 79.5 jit_solution(6629672252096884365)
XLA Ops:
  0.0 77.7 %shard_map.28 = (f32[3,4,64,1024]{3,2,1,0:T(8,128)S(1)}, f32[3,4,64,1024]{3,2,1,0:T(8,128)S(1)}) custom-call(f32[3,4,64,1024]{3,2,1,0:T(8,128)} %bitcast.7, f32[3,4,64,1024]{3,2,1,0:T(8,128)} %bitcast.8), custom_call_target="tpu_custom_call" | custom-call | tf_op jit(solution)/shard_map/pallas_call | solution.py:220
  77.7 1.8 %shard_map.29 = f32[12,64,1024]{2,1,0:T(8,128)} custom-call(f32[12,64,1024]{2,1,0:T(8,128)S(1)} %bitcast.5, f32[12,64,1024]{2,1,0:T(8,128)S(1)} %bitcast.6), custom_call_target="tpu_custom_call" | custom-call | tf_op jit(solution)/shard_map/pallas_call | solution.py:247

commit v4 on v3

--- a/solution.py
+++ b/solution.py
@@ -12,10 +12,8 @@
 TIME_DAMP = 0.5
 LANES = 256
 RING = 4
-NEAR = ((0, 1), (0, -1), (0, 2), (1, 0))
-FAR = ((1, 1), (1, -1), (1, 2))
-STEPS = NEAR + FAR
-ACROSS = (1, 0)
+STEPS = ((1, 0), (1, 1), (1, -1), (1, 2), (0, 1), (0, -1), (0, 2))
+LAST = (3, 1, 2, 0, 6, 4, 5)
 MESH = pl.DeviceIdType.MESH
 
 
@@ -62,7 +60,7 @@
 
 
 def kernel(weights, b_hbm, u_hbm, mixed, induced, field, flow, emf, got, out, edge, halo,
-           load_sem, edge_send, edge_recv, there_send, there_recv, back_send, back_recv, ready):
+           load_sem, edge_send, edge_recv, there_send, there_recv, back_send, back_recv):
     count = len(weights)
     comps, planes, rows, lanes = field.shape
     part = rows // count
@@ -77,16 +75,13 @@
         return lax.rem(moved(step) - me + count, count) - 1
 
     barrier = pltpu.get_barrier_semaphore()
-    for step in NEAR:
+    for step in STEPS:
         pl.semaphore_signal(barrier, inc=1, device_id=(moved(step), tile), device_id_type=MESH)
     for other in (before, after):
         pl.semaphore_signal(barrier, inc=1, device_id=(me, other), device_id_type=MESH)
 
     loads = [pltpu.make_async_copy(b_hbm, field, load_sem.at[0]), pltpu.make_async_copy(u_hbm, flow, load_sem.at[1])]
-    for load in loads:
-        load.start()
-    pl.semaphore_wait(barrier, len(NEAR) + 2)
-    pl.semaphore_signal(ready, inc=1, device_id=(moved(ACROSS), tile), device_id_type=MESH)
+    pl.semaphore_wait(barrier, len(STEPS) + 2)
 
     def there(z, p):
         step = STEPS[p]
@@ -104,18 +99,12 @@
             send_sem=back_send.at[z, p], recv_sem=back_recv.at[z, p],
             device_id=(moved(step), tile), device_id_type=MESH)
 
-    near, far = range(len(NEAR)), range(len(NEAR), len(STEPS))
-    for z in range(2):
-        for p in near:
-            there(z, p).start()
-    pl.semaphore_wait(ready, 1)
-    for z in range(2):
-        for p in far:
-            there(z, p).start()
-    for z in range(2, planes):
+    for z in range(planes):
         for p in range(len(STEPS)):
             there(z, p).start()
 
+    for load in loads:
+        load.start()
     for load in loads:
         load.wait()
 
@@ -157,7 +146,7 @@
             return carry
 
         lax.fori_loop(0, comps * steps, mix_block, 0)
-        for p in range(len(STEPS)):
+        for p in LAST if z == planes - 1 else range(len(STEPS)):
             back(z, p).start()
 
     lax.fori_loop(0, planes, emf_plane, 0)
@@ -237,7 +226,6 @@
             pltpu.SemaphoreType.DMA((planes, inst_count - 1)),
             pltpu.SemaphoreType.DMA((planes, inst_count - 1)),
             pltpu.SemaphoreType.DMA((planes, inst_count - 1)),
-            pltpu.SemaphoreType.REGULAR,
         ],
         compiler_params=pltpu.CompilerParams(
             collective_id=0, has_side_effects=True, vmem_limit_bytes=40 * 2**20

time: 80.3 us -> 79 us (0.984)
  Pallas kernels: 79.5 us -> 78.4 us
    pallas_call x1, Pallas kernels: 77.7 us -> 76.6 us  [per_device(): pl.pallas_call(functools.partial(kernel, time_weights(inst_count)), out_s...]
where the time goes in v4:
time: 79 us; the launch traced here: 78.4 us
  Pallas kernels  78.4 us (99%)
    pallas_call x1, Pallas kernels, per_device(): pl.pallas_call(functools.partial(kernel, time_weights(inst_count)), out_s...  76.6 us
    pallas_call x1, Pallas kernels, per_device(): pl.pallas_call(finish, out_shape=jax.ShapeDtypeStruct(flat, jnp.float32),...  1.78 us

profile of v4, /device:TPU:2, one launch (start us, length us, event | category | flops | bytes accessed | tf_op | source)
XLA Modules:
  0.0 78.4 jit_solution(11797711497836306898)
XLA Ops:
  0.0 76.6 %shard_map.28 = (f32[3,4,64,1024]{3,2,1,0:T(8,128)S(1)}, f32[3,4,64,1024]{3,2,1,0:T(8,128)S(1)}) custom-call(f32[3,4,64,1024]{3,2,1,0:T(8,128)} %bitcast.7, f32[3,4,64,1024]{3,2,1,0:T(8,128)} %bitcast.8), custom_call_target="tpu_custom_call" | custom-call | tf_op jit(solution)/shard_map/pallas_call | solution.py:209
  76.6 1.8 %shard_map.29 = f32[12,64,1024]{2,1,0:T(8,128)} custom-call(f32[12,64,1024]{2,1,0:T(8,128)S(1)} %bitcast.5, f32[12,64,1024]{2,1,0:T(8,128)S(1)} %bitcast.6), custom_call_target="tpu_custom_call" | custom-call | tf_op jit(solution)/shard_map/pallas_call | solution.py:235

commit v5 on v3

--- a/solution.py
+++ b/solution.py
@@ -12,10 +12,10 @@
 TIME_DAMP = 0.5
 LANES = 256
 RING = 4
-NEAR = ((0, 1), (0, -1), (0, 2), (1, 0))
-FAR = ((1, 1), (1, -1), (1, 2))
-STEPS = NEAR + FAR
-ACROSS = (1, 0)
+STEPS = ((1, 0), (1, 1), (1, -1), (1, 2), (0, 1), (0, -1), (0, 2))
+NEAR = (STEPS[0],) + STEPS[4:]
+LAST_ACROSS = ((2, 0, 1, 3), (0, 3, 1, 2), (0, 1, 3, 2), (1, 0, 2, 3))
+LAST_BESIDE = ((0, 2), (0, 1), (0, -1))
 MESH = pl.DeviceIdType.MESH
 
 
@@ -83,10 +83,8 @@
         pl.semaphore_signal(barrier, inc=1, device_id=(me, other), device_id_type=MESH)
 
     loads = [pltpu.make_async_copy(b_hbm, field, load_sem.at[0]), pltpu.make_async_copy(u_hbm, flow, load_sem.at[1])]
-    for load in loads:
-        load.start()
     pl.semaphore_wait(barrier, len(NEAR) + 2)
-    pl.semaphore_signal(ready, inc=1, device_id=(moved(ACROSS), tile), device_id_type=MESH)
+    pl.semaphore_signal(ready, inc=1, device_id=(moved((1, 0)), tile), device_id_type=MESH)
 
     def there(z, p):
         step = STEPS[p]
@@ -97,25 +95,34 @@
 
     own = pl.ds(pl.multiple_of(me * part, part), part)
 
+    def last_step(p):
+        if p >= RING:
+            return LAST_BESIDE[p - RING]
+        spot, place = me % RING, LAST_ACROSS[-1][p]
+        for at in range(RING - 1):
+            place = jnp.where(spot == at, LAST_ACROSS[at][p], place)
+        return (1, place - spot)
+
     def back(z, p):
-        step = STEPS[p]
+        step = last_step(p) if z == planes - 1 else STEPS[p]
         return pltpu.make_async_remote_copy(
             src_ref=out.at[slot(step), z], dst_ref=mixed.at[:, z, own, :],
-            send_sem=back_send.at[z, p], recv_sem=back_recv.at[z, p],
+            send_sem=back_send.at[z, p], recv_sem=back_recv.at[z, slot(step)],
             device_id=(moved(step), tile), device_id_type=MESH)
 
-    near, far = range(len(NEAR)), range(len(NEAR), len(STEPS))
     for z in range(2):
-        for p in near:
+        for p in (0, 4, 5, 6):
             there(z, p).start()
     pl.semaphore_wait(ready, 1)
     for z in range(2):
-        for p in far:
+        for p in (1, 2, 3):
             there(z, p).start()
     for z in range(2, planes):
         for p in range(len(STEPS)):
             there(z, p).start()
 
+    for load in loads:
+        load.start()
     for load in loads:
         load.wait()
 

time: 80.3 us -> 78.3 us (0.975)
  Pallas kernels: 79.5 us -> 78.1 us
    pallas_call x1, Pallas kernels: 77.7 us -> 76.3 us  [per_device(): pl.pallas_call(functools.partial(kernel, time_weights(inst_count)), out_s...]
where the time goes in v5:
time: 78.3 us; the launch traced here: 78.1 us
  Pallas kernels  78.1 us (100%)
    pallas_call x1, Pallas kernels, per_device(): pl.pallas_call(functools.partial(kernel, time_weights(inst_count)), out_s...  76.3 us
    pallas_call x1, Pallas kernels, per_device(): pl.pallas_call(finish, out_shape=jax.ShapeDtypeStruct(flat, jnp.float32),...  1.78 us

profile of v5, /device:TPU:2, one launch (start us, length us, event | category | flops | bytes accessed | tf_op | source)
XLA Modules:
  0.0 78.1 jit_solution(16719168445947750723)
XLA Ops:
  0.0 76.3 %shard_map.28 = (f32[3,4,64,1024]{3,2,1,0:T(8,128)S(1)}, f32[3,4,64,1024]{3,2,1,0:T(8,128)S(1)}) custom-call(f32[3,4,64,1024]{3,2,1,0:T(8,128)} %bitcast.7, f32[3,4,64,1024]{3,2,1,0:T(8,128)} %bitcast.8), custom_call_target="tpu_custom_call" | custom-call | tf_op jit(solution)/shard_map/pallas_call | solution.py:227
  76.3 1.8 %shard_map.29 = f32[12,64,1024]{2,1,0:T(8,128)} custom-call(f32[12,64,1024]{2,1,0:T(8,128)S(1)} %bitcast.5, f32[12,64,1024]{2,1,0:T(8,128)S(1)} %bitcast.6), custom_call_target="tpu_custom_call" | custom-call | tf_op jit(solution)/shard_map/pallas_call | solution.py:254

commit v6 on v5

--- a/solution.py
+++ b/solution.py
@@ -11,6 +11,8 @@
 RESIST = 0.2
 TIME_DAMP = 0.5
 LANES = 256
+PIECES = ((0, 2), (2, 1), (3, 1))
+EARLY = 1
 RING = 4
 STEPS = ((1, 0), (1, 1), (1, -1), (1, 2), (0, 1), (0, -1), (0, 2))
 NEAR = (STEPS[0],) + STEPS[4:]
@@ -86,11 +88,11 @@
     pl.semaphore_wait(barrier, len(NEAR) + 2)
     pl.semaphore_signal(ready, inc=1, device_id=(moved((1, 0)), tile), device_id_type=MESH)
 
-    def there(z, p):
-        step = STEPS[p]
+    def there(q, p):
+        step, at = STEPS[p], pl.ds(*PIECES[q])
         return pltpu.make_async_remote_copy(
-            src_ref=b_hbm.at[:, z, pl.ds(pl.multiple_of(moved(step) * part, part), part), :], dst_ref=got.at[slot(step), z],
-            send_sem=there_send.at[z, p], recv_sem=there_recv.at[z, p],
+            src_ref=b_hbm.at[:, at, pl.ds(pl.multiple_of(moved(step) * part, part), part), :], dst_ref=got.at[slot(step), :, at],
+            send_sem=there_send.at[q, p], recv_sem=there_recv.at[q, p],
             device_id=(moved(step), tile), device_id_type=MESH)
 
     own = pl.ds(pl.multiple_of(me * part, part), part)
@@ -103,23 +105,23 @@
             place = jnp.where(spot == at, LAST_ACROSS[at][p], place)
         return (1, place - spot)
 
-    def back(z, p):
-        step = last_step(p) if z == planes - 1 else STEPS[p]
+    def back(q, p):
+        step, at = last_step(p) if q == len(PIECES) - 1 else STEPS[p], pl.ds(*PIECES[q])
         return pltpu.make_async_remote_copy(
-            src_ref=out.at[slot(step), z], dst_ref=mixed.at[:, z, own, :],
-            send_sem=back_send.at[z, p], recv_sem=back_recv.at[z, slot(step)],
+            src_ref=out.at[slot(step), :, at], dst_ref=mixed.at[:, at, own, :],
+            send_sem=back_send.at[q, p], recv_sem=back_recv.at[q, slot(step)],
             device_id=(moved(step), tile), device_id_type=MESH)
 
-    for z in range(2):
+    for q in range(EARLY):
         for p in (0, 4, 5, 6):
-            there(z, p).start()
+            there(q, p).start()
     pl.semaphore_wait(ready, 1)
-    for z in range(2):
+    for q in range(EARLY):
         for p in (1, 2, 3):
-            there(z, p).start()
-    for z in range(2, planes):
-        for p in range(len(STEPS)):
-            there(z, p).start()
+            there(q, p).start()
+    for q in range(EARLY, len(PIECES)):
+        for p in range(len(STEPS)):
+            there(q, p).start()
 
     for load in loads:
         load.start()
@@ -150,22 +152,22 @@
         return carry
 
     steps = lanes // LANES
-    for z in range(planes):
-        for p in range(len(STEPS)):
-            there(z, p).wait_recv()
-
-        def mix_block(i, carry, z=z):
-            c, at = i // steps, pl.ds(pl.multiple_of((i % steps) * LANES, LANES), LANES)
-            fields = [field[c, z, own, at]] + [got[k, z, c, :, at] for k in range(count - 1)]
+    for q, (first, depth) in enumerate(PIECES):
+        for p in range(len(STEPS)):
+            there(q, p).wait_recv()
+
+        def mix_block(i, carry, first=first):
+            z, c, at = first + i // (comps * steps), i // steps % comps, pl.ds(pl.multiple_of((i % steps) * LANES, LANES), LANES)
+            fields = [field[c, z, own, at]] + [got[k, c, z, :, at] for k in range(count - 1)]
             values = mix(fields, weights)
             mixed[c, z, own, at] = values[0]
             for k in range(1, count):
-                out[k - 1, z, c, :, at] = values[k]
+                out[k - 1, c, z, :, at] = values[k]
             return carry
 
-        lax.fori_loop(0, comps * steps, mix_block, 0)
-        for p in range(len(STEPS)):
-            back(z, p).start()
+        lax.fori_loop(0, depth * comps * steps, mix_block, 0)
+        for p in range(len(STEPS)):
+            back(q, p).start()
 
     lax.fori_loop(0, planes, emf_plane, 0)
 
@@ -201,10 +203,10 @@
 
     lax.fori_loop(0, planes, induction_plane, 0)
 
-    for z in range(planes):
-        for p in range(len(STEPS)):
-            there(z, p).wait_send()
-            back(z, p).wait()
+    for q in range(len(PIECES)):
+        for p in range(len(STEPS)):
+            there(q, p).wait_send()
+            back(q, p).wait()
 
 
 def finish(mixed, induced, result, block, sem):
@@ -233,17 +235,17 @@
             pltpu.VMEM(shape, jnp.float32),
             pltpu.VMEM(shape, jnp.float32),
             pltpu.VMEM(shape, jnp.float32),
-            pltpu.VMEM((inst_count - 1, planes, comps, part, lanes), jnp.float32),
-            pltpu.VMEM((inst_count - 1, planes, comps, part, lanes), jnp.float32),
+            pltpu.VMEM((inst_count - 1, comps, planes, part, lanes), jnp.float32),
+            pltpu.VMEM((inst_count - 1, comps, planes, part, lanes), jnp.float32),
             pltpu.VMEM((2, comps * planes, lanes), jnp.float32),
             pltpu.VMEM((2, comps * planes, lanes), jnp.float32),
             pltpu.SemaphoreType.DMA((2,)),
             pltpu.SemaphoreType.DMA((2,)),
             pltpu.SemaphoreType.DMA((2,)),
-            pltpu.SemaphoreType.DMA((planes, inst_count - 1)),
-            pltpu.SemaphoreType.DMA((planes, inst_count - 1)),
-            pltpu.SemaphoreType.DMA((planes, inst_count - 1)),
-            pltpu.SemaphoreType.DMA((planes, inst_count - 1)),
+            pltpu.SemaphoreType.DMA((len(PIECES), inst_count - 1)),
+            pltpu.SemaphoreType.DMA((len(PIECES), inst_count - 1)),
+            pltpu.SemaphoreType.DMA((len(PIECES), inst_count - 1)),
+            pltpu.SemaphoreType.DMA((len(PIECES), inst_count - 1)),
             pltpu.SemaphoreType.REGULAR,
         ],
         compiler_params=pltpu.CompilerParams(

time: 78.3 us -> 78.2 us (level)
  no operation moved by 1% of the time
where the time goes in v6:
time: 78.2 us; the launch traced here: 77.9 us
  Pallas kernels  77.9 us (100%)
    pallas_call x1, Pallas kernels, per_device(): pl.pallas_call(functools.partial(kernel, time_weights(inst_count)), out_s...  76.1 us
    pallas_call x1, Pallas kernels, per_device(): pl.pallas_call(finish, out_shape=jax.ShapeDtypeStruct(flat, jnp.float32),...  1.78 us

profile of v6, /device:TPU:2, one launch (start us, length us, event | category | flops | bytes accessed | tf_op | source)
XLA Modules:
  0.0 77.9 jit_solution(15339196502083122987)
XLA Ops:
  0.0 76.1 %shard_map.28 = (f32[3,4,64,1024]{3,2,1,0:T(8,128)S(1)}, f32[3,4,64,1024]{3,2,1,0:T(8,128)S(1)}) custom-call(f32[3,4,64,1024]{3,2,1,0:T(8,128)} %bitcast.7, f32[3,4,64,1024]{3,2,1,0:T(8,128)} %bitcast.8), custom_call_target="tpu_custom_call" | custom-call | tf_op jit(solution)/shard_map/pallas_call | solution.py:229
  76.1 1.8 %shard_map.29 = f32[12,64,1024]{2,1,0:T(8,128)} custom-call(f32[12,64,1024]{2,1,0:T(8,128)S(1)} %bitcast.5, f32[12,64,1024]{2,1,0:T(8,128)S(1)} %bitcast.6), custom_call_target="tpu_custom_call" | custom-call | tf_op jit(solution)/shard_map/pallas_call | solution.py:256

commit v7 on v6

--- a/solution.py
+++ b/solution.py
@@ -11,7 +11,7 @@
 RESIST = 0.2
 TIME_DAMP = 0.5
 LANES = 256
-PIECES = ((0, 2), (2, 1), (3, 1))
+PIECES = ((0, 1), (1, 2), (3, 1))
 EARLY = 1
 RING = 4
 STEPS = ((1, 0), (1, 1), (1, -1), (1, 2), (0, 1), (0, -1), (0, 2))

time: 78.2 us -> 78.1 us (level)
  no operation moved by 1% of the time
where the time goes in v7:
time: 78.1 us; the launch traced here: 77.9 us
  Pallas kernels  77.9 us (100%)
    pallas_call x1, Pallas kernels, per_device(): pl.pallas_call(functools.partial(kernel, time_weights(inst_count)), out_s...  76.1 us
    pallas_call x1, Pallas kernels, per_device(): pl.pallas_call(finish, out_shape=jax.ShapeDtypeStruct(flat, jnp.float32),...  1.78 us

profile of v7, /device:TPU:2, one launch (start us, length us, event | category | flops | bytes accessed | tf_op | source)
XLA Modules:
  0.0 77.9 jit_solution(2575898451870921102)
XLA Ops:
  0.0 76.1 %shard_map.28 = (f32[3,4,64,1024]{3,2,1,0:T(8,128)S(1)}, f32[3,4,64,1024]{3,2,1,0:T(8,128)S(1)}) custom-call(f32[3,4,64,1024]{3,2,1,0:T(8,128)} %bitcast.7, f32[3,4,64,1024]{3,2,1,0:T(8,128)} %bitcast.8), custom_call_target="tpu_custom_call" | custom-call | tf_op jit(solution)/shard_map/pallas_call | solution.py:229
  76.1 1.8 %shard_map.29 = f32[12,64,1024]{2,1,0:T(8,128)} custom-call(f32[12,64,1024]{2,1,0:T(8,128)S(1)} %bitcast.5, f32[12,64,1024]{2,1,0:T(8,128)S(1)} %bitcast.6), custom_call_target="tpu_custom_call" | custom-call | tf_op jit(solution)/shard_map/pallas_call | solution.py:256
